TPU v7x, 32 devices: a whole 2x2x4 slice. The times are simulated.
32 devices in a mesh: groups: 2 (over x), gx: 16 (over z, y, core).
Axes of the slice: x: 2, y: 2, z: 4, core: 2. Of those that a mesh axis runs over, the one named last changes fastest.
Arguments:
- inputs: bfloat16 [16, 256, 6144], P('gx', 'groups'), parts along dimension 1, may hold values from -6 to 6
- weight: bfloat16 [16, 12288, 3072], P('gx', 'groups'), parts along dimension 1, may hold values from -0.0546875 to 0.0546875
- preact: bfloat16 [16, 1024, 3072], P('gx', 'groups'), parts along dimension 1, may hold values from -6 to 6
- out_grad: bfloat16 [16, 1024, 3072], P('gx', 'groups'), parts along dimension 1, may hold values from -4 to 4
Outputs:
- in_grad: bfloat16 [16, 256, 6144], P('gx', 'groups'), parts along dimension 1
- weight_grad: bfloat16 [16, 12288, 3072], P('gx', 'groups'), parts along dimension 1
There are 2 independent parts, one for each index of `groups`. A program takes and returns all parts, laid end to end along the dimension named above; each array names one. Nothing has to cross between parts.
All inputs are finite; a program needn't handle non-finite values.
Results may differ from a plain program's by a relative error of at most 0.0049.
Values may be sent and summed in bfloat16 or wider, within the bound.
A program may use at most 256 MiB of HBM per device.

v0:
```python
import math

import jax
import jax.numpy as jnp
from jax import lax
from jax.sharding import PartitionSpec as P

GC = 8


def partner_2(array, axis, distance):
    return lax.ppermute(array, axis, [(i, i ^ 1 << distance) for i in range(lax.axis_size(axis))])


def gelu_slope(gradient, preact):
    value = preact.astype(jnp.float32)
    coeff = math.sqrt(2.0 / math.pi)
    inner = coeff * (value + 0.044715 * value * value * value)
    tangent = jnp.tanh(inner)
    slope = 0.5 * (1.0 + tangent) + 0.5 * value * (1.0 - tangent * tangent) * coeff * (
        1.0 + 3.0 * 0.044715 * value * value
    )
    return (gradient.astype(jnp.float32) * slope).astype(jnp.bfloat16)


def on_device(inputs, weight, preact, out_grad):
    col_bits = GC.bit_length() - 1
    total_bits = lax.axis_size("gx").bit_length() - 1
    device_index = lax.axis_index("gx")
    x_block = inputs[0]
    w_block = weight[0]
    stacked = jnp.stack([out_grad[0], preact[0]])
    for bit_pos in range(col_bits, total_bits):
        partner = partner_2(stacked, "gx", bit_pos)
        my_bit = device_index // (1 << bit_pos) % 2
        stacked = jnp.where(
            my_bit == 0,
            jnp.concatenate([stacked, partner], 1),
            jnp.concatenate([partner, stacked], 1),
        )
    dy_all = gelu_slope(stacked[0], stacked[1])
    x_all = x_block
    for bit_pos in range(col_bits):
        partner = partner_2(x_all, "gx", bit_pos)
        my_bit = device_index // (1 << bit_pos) % 2
        x_all = jnp.where(
            my_bit == 0, jnp.concatenate([x_all, partner], 0), jnp.concatenate([partner, x_all], 0)
        )
    weight_grad = lax.dot_general(
        x_all, dy_all, (((0,), (0,)), ((), ())), preferred_element_type=jnp.float32
    )
    partial_value = lax.dot_general(
        dy_all, w_block, (((1,), (1,)), ((), ())), preferred_element_type=jnp.float32
    )
    for bit_pos in reversed(range(col_bits)):
        half_rows = partial_value.shape[0] // 2
        lower_rows = partial_value[:half_rows]
        upper_rows = partial_value[half_rows:]
        my_bit = device_index // (1 << bit_pos) % 2
        outgoing = jnp.where(my_bit == 1, lower_rows, upper_rows)
        kept_rows = jnp.where(my_bit == 1, upper_rows, lower_rows)
        partial_value = kept_rows + partner_2(outgoing, "gx", bit_pos)
    return (partial_value.astype(jnp.bfloat16)[None], weight_grad.astype(jnp.bfloat16)[None])


def solution(mesh):
    return jax.shard_map(
        on_device,
        mesh=mesh,
        in_specs=(
            P("gx", "groups", None),
            P("gx", "groups", None),
            P("gx", "groups", None),
            P("gx", "groups", None),
        ),
        out_specs=(P("gx", "groups", None), P("gx", "groups", None)),
        check_vma=False,
    )
```

profile of v0, /device:TPU:0, one launch (start us, length us, event | category | flops | bytes accessed | tf_op | source)
XLA Modules:
  0.0 858.7 jit_solution(15411951025314965466)
XLA Ops:
  0.6 3.8 constant_dynamic-update-slice_fusion.1
  4.4 3.8 constant_dynamic-update-slice_fusion
  8.1 4.0 collective-permute-start
  12.2 270.6 %collective-permute-done = bf16[2,512,3072]{2,1,0:T(8,128)(2,1)} collective-permute-done((bf16[2,512,3072]{2,1,0:T(8,128)(2,1)}, bf16[2,512,3072]{2,1,0:T(8,128)(2,1)}, u32[]{:S(2)}, u32[]{:S(2)}) %collective-permute-start) | collective-permute-done | bytes 6291488 | tf_op jit(solution)/shard_map/ppermute | solution.py:12
  282.8 11.7 %maximum_select_fusion = bf16[2,1024,3072]{2,1,0:T(8,128)(2,1)S(1)} fusion(bf16[2,512,3072]{2,1,0:T(8,128)(2,1)} %collective-permute-done, bf16[2,512,3072]{2,1,0:T(8,128)(2,1)} %constant_dynamic-update-slice_fusion, pred[]{:T(512)S(6)} %eq.35), kind=kLoop, calls=%fused_computation.37 | loop fusion | flops 56623104 | bytes 25165824 | tf_op jit(solution)/shard_map/jit(_where)/select_n | solution.py:36
  294.6 0.0 copy-start
  294.6 4.5 copy-done
  299.1 8.8 %fusion.66 = bf16[1024,3072]{1,0:T(8,128)(2,1)S(1)} fusion(bf16[2,1024,3072]{2,1,0:T(8,128)(2,1)S(1)} %maximum_select_fusion), kind=kLoop, calls=%fused_computation.48.clone.1 | loop fusion | flops 66060288 | bytes 18874368 | tf_op jit(solution)/shard_map/dot_general | solution.py:52
  307.9 45.0 %fusion = f32[1024,6144]{1,0:T(8,128)} fusion(bf16[1,6144,3072]{2,1,0:T(8,128)(2,1)} %param.5, bf16[1024,3072]{1,0:T(8,128)(2,1)S(1)} %fusion.66), kind=kOutput, calls=%fused_computation | convolution fusion | flops 38654705664 | bytes 69206016 | tf_op jit(solution)/shard_map/dot_general | solution.py:52
  352.9 0.0 copy-start.2
  352.9 14.5 %slice_select_fusion = f32[512,6144]{1,0:T(8,128)} fusion(f32[1024,6144]{1,0:T(8,128)} %fusion, pred[]{:T(512)S(6)} %eq.34), kind=kLoop, calls=%fused_computation.46 | loop fusion | flops 3145728 | bytes 37748736 | tf_op jit(solution)/shard_map/jit(_where)/select_n | solution.py:60
  367.4 0.7 collective-permute-start.1
  368.1 0.0 copy-done.2
  368.1 0.0 collective-permute-start.4
  368.1 3.5 collective-permute-done.4
  371.7 3.4 maximum_select_fusion.4
  375.1 1.6 collective-permute-start.5
  376.7 262.5 %collective-permute-done.1 = f32[512,6144]{1,0:T(8,128)} collective-permute-done((f32[512,6144]{1,0:T(8,128)}, f32[512,6144]{1,0:T(8,128)}, u32[]{:S(2)}, u32[]{:S(2)}) %collective-permute-start.1) | collective-permute-done | bytes 12582944 | tf_op jit(solution)/shard_map/ppermute | solution.py:12
  639.2 13.4 %select_add_fusion = f32[512,6144]{1,0:T(8,128)S(1)} fusion(f32[512,6144]{1,0:T(8,128)} %collective-permute-done.1, f32[1024,6144]{1,0:T(8,128)} %fusion, pred[]{:T(512)S(6)} %eq.34), kind=kLoop, calls=%fused_computation.44 | loop fusion | flops 6291456 | bytes 50331648 | tf_op jit(solution)/shard_map/add | solution.py:62
  652.6 0.0 copy-start.1
  652.7 4.8 copy-done.1
  657.4 3.5 slice_select_fusion.1
  660.9 1.3 collective-permute-start.2
  662.2 0.0 collective-permute-done.5
  662.2 7.7 maximum_select_fusion.3
  669.9 1.7 collective-permute-start.6
  671.6 12.4 %fusion.68 = bf16[1024,3072]{1,0:T(8,128)(2,1)} fusion(bf16[2,1024,3072]{2,1,0:T(8,128)(2,1)} %copy-done), kind=kLoop, calls=%fused_computation.22.clone.clone.2 | loop fusion | flops 66060288 | bytes 18874368 | tf_op jit(solution)/shard_map/dot_general | solution.py:49
  684.0 113.0 %collective-permute-done.2 = f32[256,6144]{1,0:T(8,128)} collective-permute-done((f32[256,6144]{1,0:T(8,128)}, f32[256,6144]{1,0:T(8,128)}, u32[]{:S(2)}, u32[]{:S(2)}) %collective-permute-start.2) | collective-permute-done | bytes 6291488 | tf_op jit(solution)/shard_map/ppermute | solution.py:12
  797.0 7.9 select_add_fusion.1
  804.9 2.0 slice_select_fusion.2
  806.9 0.0 collective-permute-start.3
  806.9 0.0 collective-permute-done.6
  806.9 48.2 %convert_bitcast_fusion = bf16[1,6144,3072]{2,1,0:T(8,128)(2,1)} fusion(bf16[512,6144]{1,0:T(8,128)(2,1)} %collective-permute-done.6, bf16[512,6144]{1,0:T(8,128)(2,1)} %maximum_select_fusion.3, pred[]{:T(512)S(6)} %eq.36, bf16[1024,3072]{1,0:T(8,128)(2,1)} %fusion.68), kind=kOutput, calls=%fused_computation.2 | convolution fusion | flops 38730203136 | bytes 56623104 | tf_op jit(solution)/shard_map/dot_general | solution.py:49
  855.1 0.0 collective-permute-done.3
  855.1 3.6 fusion.48
Async XLA Ops:
  8.1 274.7 %collective-permute-start = (bf16[2,512,3072]{2,1,0:T(8,128)(2,1)}, bf16[2,512,3072]{2,1,0:T(8,128)(2,1)}, u32[]{:S(2)}, u32[]{:S(2)}) collective-permute-start(bf16[2,512,3072]{2,1,0:T(8,128)(2,1)} %constant_dynamic-update-slice_fusion), channel_id=1, source_target_pairs={{0,8},{1,9},{2,10},{3,11},{4,12},{5,13},{6,14},{7,15},{8,0},{9,1},... | collective-permute-start | bytes 18874376 | tf_op jit(solution)/shard_map/ppermute | solution.py:12
  294.6 4.5 copy-start
  352.9 15.2 %copy-start.2 = (bf16[1,128,6144]{2,1,0:T(8,128)(2,1)S(1)}, bf16[1,128,6144]{2,1,0:T(8,128)(2,1)}, u32[]{:S(2)}) copy-start(bf16[1,128,6144]{2,1,0:T(8,128)(2,1)} %param.4) | copy-start | bytes 4718596
  367.4 271.8 %collective-permute-start.1 = (f32[512,6144]{1,0:T(8,128)}, f32[512,6144]{1,0:T(8,128)}, u32[]{:S(2)}, u32[]{:S(2)}) collective-permute-start(f32[512,6144]{1,0:T(8,128)} %slice_select_fusion), channel_id=1, source_target_pairs={{0,4},{1,5},{2,6},{3,7},{4,0},{5,1},{6,2},{7,3},{8,12},{9,13},{10,... | collective-permute-start | bytes 37748744 | tf_op jit(solution)/shard_map/ppermute | solution.py:12
  368.1 3.5 collective-permute-start.4
  375.1 287.0 %collective-permute-start.5 = (bf16[256,6144]{1,0:T(8,128)(2,1)S(1)}, bf16[256,6144]{1,0:T(8,128)(2,1)}, u32[]{:S(2)}, u32[]{:S(2)}) collective-permute-start(bf16[256,6144]{1,0:T(8,128)(2,1)S(1)} %maximum_select_fusion.4), channel_id=1, source_target_pairs={{0,2},{1,3},{2,0},{3,1},{4,6},{5,7},{6,4},{7,5},{8,10},{9,11},{10,... | collective-permute-start | bytes 9437192 | tf_op jit(solution)/shard_map/ppermute | solution.py:12
  652.6 4.8 copy-start.1
  660.9 136.1 %collective-permute-start.2 = (f32[256,6144]{1,0:T(8,128)}, f32[256,6144]{1,0:T(8,128)}, u32[]{:S(2)}, u32[]{:S(2)}) collective-permute-start(f32[256,6144]{1,0:T(8,128)} %slice_select_fusion.1), channel_id=1, source_target_pairs={{0,2},{1,3},{2,0},{3,1},{4,6},{5,7},{6,4},{7,5},{8,10},{9,11},{10,... | collective-permute-start | bytes 18874376 | tf_op jit(solution)/shard_map/ppermute | solution.py:12
  669.9 137.0 %collective-permute-start.6 = (bf16[512,6144]{1,0:T(8,128)(2,1)}, bf16[512,6144]{1,0:T(8,128)(2,1)}, u32[]{:S(2)}, u32[]{:S(2)}) collective-permute-start(bf16[512,6144]{1,0:T(8,128)(2,1)} %maximum_select_fusion.3), channel_id=1, source_target_pairs={{0,4},{1,5},{2,6},{3,7},{4,0},{5,1},{6,2},{7,3},{8,12},{9,13},{10,... | collective-permute-start | bytes 18874376 | tf_op jit(solution)/shard_map/ppermute | solution.py:12
  806.9 48.2 %collective-permute-start.3 = (f32[128,6144]{1,0:T(8,128)}, f32[128,6144]{1,0:T(8,128)}, u32[]{:S(2)}, u32[]{:S(2)}) collective-permute-start(f32[128,6144]{1,0:T(8,128)} %slice_select_fusion.2), channel_id=1, source_target_pairs={{0,1},{1,0},{2,3},{3,2},{4,5},{5,4},{6,7},{7,6},{8,9},{9,8},{10,11... | collective-permute-start | bytes 9437192 | tf_op jit(solution)/shard_map/ppermute | solution.py:12
where the time goes:
time: 860 us; the launch traced here: 859 us
  waiting for transfers between devices  650 us (76%)
  matrix products  93.2 us (11%)
  other arithmetic  89 us (10%)
  local copies, waits for them, and re-layouts  16.8 us (2%)
  starting transfers between devices  9.33 us (1%)
    ppermute x7, waiting for transfers between devices, partner_2(): lax.ppermute(array, axis, [(i, i ^ 1 << distance) for i in range(lax.axis...  650 us
    dot_general x1, matrix products, on_device(): lax.dot_general(x_all, dy_all, (((0,), (0,)), ((), ())), preferred_elemen...  48.2 us
    dot_general x1, matrix products, on_device(): lax.dot_general(dy_all, w_block, (((1,), (1,)), ((), ())), preferred_elem...  45 us
    add x2, other arithmetic, on_device(): partial_value = kept_rows + partner_2(outgoing, 'gx', bit_pos)  21.3 us
    select_n x3, other arithmetic, on_device(): outgoing = jnp.where(my_bit == 1, lower_rows, upper_rows)  19.9 us
  transfers between devices with their start and end apart: 7, of which 4 were waited for; matrix products, arithmetic and copies ran while one was open for 11% of the time, Pallas kernels for 0%

commit v1 on v0

v1 whole, which is shorter than its diff:
```python
import math

import jax
import jax.numpy as jnp
from jax import lax
from jax.sharding import PartitionSpec as P

GC = 8
CHUNKS = 4
F32 = jnp.float32
BF16 = jnp.bfloat16


def gelu_slope(gradient, preact):
    value = preact.astype(F32)
    coeff = math.sqrt(2.0 / math.pi)
    inner = coeff * (value + 0.044715 * value * value * value)
    tangent = jnp.tanh(inner)
    slope = 0.5 * (1.0 + tangent) + 0.5 * value * (1.0 - tangent * tangent) * coeff * (
        1.0 + 3.0 * 0.044715 * value * value
    )
    return (gradient.astype(F32) * slope).astype(BF16)


def swap(array, distance):
    size = lax.axis_size("gx")
    return lax.ppermute(array, "gx", [(i, i ^ distance) for i in range(size)])


def join(bit, own, other, axis):
    low = jnp.where(bit == 0, own, other)
    high = jnp.where(bit == 0, other, own)
    return jnp.concatenate([low, high], axis)


def times_wt(rows, w):
    return lax.dot_general(rows, w, (((1,), (1,)), ((), ())), preferred_element_type=F32)


def xt_times(x, dy):
    return lax.dot_general(x, dy, (((0,), (0,)), ((), ())), preferred_element_type=F32)


def take(array, index, axis):
    return lax.dynamic_index_in_dim(array, index, axis, keepdims=False)


def general(index, x, w, preact, out_grad):
    size = lax.axis_size("gx")
    dy = gelu_slope(out_grad, preact)
    distance = GC
    while distance < size:
        dy = join(index // distance % 2, dy, swap(dy, distance), 0)
        distance *= 2
    x_all = x[None]
    for distance in (4, 2, 1):
        bit = index // distance % 2
        x_all = join(bit, x_all, swap(x_all, distance), 0)
    tokens, width = x.shape
    x_all = x_all.reshape(2, 2, 2, tokens, width).transpose(2, 1, 0, 3, 4).reshape(-1, width)
    weight_grad = xt_times(x_all, dy).astype(BF16)
    part = times_wt(dy, w).reshape(2, 2, 2, tokens, -1)
    for distance, axis in ((1, 2), (2, 1), (4, 0)):
        bit = index // distance % 2
        kept = take(part, bit, axis)
        sent = take(part, 1 - bit, axis).astype(BF16)
        part = kept + swap(sent, distance).astype(F32)
    return part.astype(BF16), weight_grad


def two_rows(index, x, w, preact, out_grad):
    row, z, y, core = index // GC, index // 4 % 2, index // 2 % 2, index % 2
    tokens, width = x.shape
    hidden = w.shape[1]
    step = tokens // CHUNKS
    mine = z == row

    g4, p4 = out_grad.reshape(4, tokens, hidden), preact.reshape(4, tokens, hidden)
    dy_own, dy_other = [], []
    for q in range(CHUNKS):
        part = slice(q * step, (q + 1) * step)
        dy_own.append(gelu_slope(g4[:, part], p4[:, part]).reshape(4 * step, hidden))
        dy_other.append(swap(dy_own[-1], GC))

    partner = swap(x, 4)
    x_own, x_other = jnp.where(mine, x, partner), jnp.where(mine, partner, x)

    def spread(piece):
        piece = join(y, piece[None], swap(piece, 2)[None], 0)
        piece = join(core, piece[:, None], swap(piece, 1)[:, None], 1)
        return piece.reshape(4 * tokens, width)

    def order(chunks):
        return jnp.concatenate([c.reshape(4, step, hidden) for c in chunks], 1).reshape(
            4 * tokens, hidden
        )

    def reduce(part):
        part = part.reshape(2, 2, -1, part.shape[-1])
        part = take(part, core, 1).astype(F32) + swap(take(part, 1 - core, 1), 1).astype(F32)
        sent = take(part, 1 - y, 0).astype(BF16)
        return take(part, y, 0) + swap(sent, 2).astype(F32)

    size = lax.axis_size("gx")
    to_own = [(i, i ^ 4) for i in range(size) if i // 4 % 2 != i // GC]
    to_other = [(i, i ^ 4) for i in range(size) if i // 4 % 2 == i // GC]

    def last(piece, pairs):
        return piece, lax.ppermute(piece.astype(BF16), "gx", pairs)

    own_rows = order(dy_own)
    half = width // 2
    own_sum, own_recv = [], []
    for h in range(2):
        part = times_wt(own_rows, w[h * half : (h + 1) * half]).astype(BF16)
        kept, recv = last(reduce(part), to_own)
        own_sum.append(kept)
        own_recv.append(recv)
    own_sum, own_recv = jnp.concatenate(own_sum, 1), jnp.concatenate(own_recv, 1)

    dw_own = xt_times(spread(x_own), own_rows).astype(BF16)

    outs = []
    for q in range(CHUNKS):
        kept, recv = last(reduce(times_wt(dy_other[q], w).astype(BF16)), to_other)
        part = slice(q * step, (q + 1) * step)
        outs.append(
            jnp.where(
                mine,
                own_sum[part] + own_recv[part].astype(F32),
                kept + recv.astype(F32),
            ).astype(BF16)
        )
    weight_grad = (dw_own.astype(F32) + xt_times(spread(x_other), order(dy_other))).astype(BF16)
    return jnp.concatenate(outs, 0), weight_grad


def on_device(inputs, weight, preact, out_grad):
    index = lax.axis_index("gx")
    run = two_rows if lax.axis_size("gx") == 2 * GC else general
    in_grad, weight_grad = run(index, inputs[0], weight[0], preact[0], out_grad[0])
    return in_grad[None], weight_grad[None]


def solution(mesh):
    spec = P("gx", "groups", None)
    return jax.shard_map(
        on_device,
        mesh=mesh,
        in_specs=(spec,) * 4,
        out_specs=(spec, spec),
        check_vma=False,
    )
```

time: 860 us -> 449 us (0.52)
  waiting for transfers between devices: 650 us -> 195 us
  matrix products: 93.2 us -> 164 us
  other arithmetic: 89 us -> 32.6 us
  starting transfers between devices: 9.33 us -> 31.9 us
    ppermute x7 -> x27, waiting for transfers between devices: 650 us -> 195 us  [the longest x21 183 us: swap(): return lax.ppermute(array, 'gx', [(i, i ^ distance) for i in range(size)])]
    dot_general x2 -> x8, matrix products: 93.2 us -> 164 us  [the longest x6 102 us: times_wt(): lax.dot_general(rows, w, (((1,), (1,)), ((), ())), preferred_element_type...]
    select_n x6 -> x5, other arithmetic: 42.8 us -> 4.84 us  [the longest x4 3.22 us: join(): low = jnp.where(bit == 0, own, other)]
    ppermute x7 -> x27, starting transfers between devices: 9.33 us -> 31.9 us  [the longest x21 18.9 us: swap(): return lax.ppermute(array, 'gx', [(i, i ^ distance) for i in range(size)])]
    dot_general x2 -> x0, other arithmetic: 21.2 us -> none  [the longest x1 12.4 us: on_device(): lax.dot_general(x_all, dy_all, (((0,), (0,)), ((), ())), preferred_elemen...]
    add x2 -> x6, other arithmetic: 21.3 us -> 6.75 us  [reduce(): take(part, core, 1).astype(F32)]
    concatenate x0 -> x6, other arithmetic: none -> 11 us  [the longest x4 6.01 us: join(): return jnp.concatenate([low, high], axis)]
    convert_element_type x0 -> x9, other arithmetic: none -> 8.78 us  [the longest x1 7.16 us: gelu_slope(): return (gradient.astype(F32) * slope).astype(BF16)]
  transfers between devices with their start and end apart: 7 -> 27, of which waited for: 4 -> 10; matrix products, arithmetic and copies ran while one was open for 11% -> 32% of each run, Pallas kernels for 0% -> 0%
where the time goes in v1:
time: 449 us; the launch traced here: 440 us
  waiting for transfers between devices  195 us (43%)
  matrix products  164 us (37%)
  other arithmetic  32.6 us (7%)
  starting transfers between devices  31.9 us (7%)
  local copies, waits for them, and re-layouts  15 us (3%)
    ppermute x21, waiting for transfers between devices, swap(): return lax.ppermute(array, 'gx', [(i, i ^ distance) for i in range(size)])  183 us
    dot_general x6, matrix products, times_wt(): lax.dot_general(rows, w, (((1,), (1,)), ((), ())), preferred_element_type...  102 us
    dot_general x2, matrix products, xt_times(): lax.dot_general(x, dy, (((0,), (0,)), ((), ())), preferred_element_type=F32)  61.9 us
    ppermute x21, starting transfers between devices, swap(): return lax.ppermute(array, 'gx', [(i, i ^ distance) for i in range(size)])  18.9 us
    ppermute x6, starting transfers between devices, last(): return (piece, lax.ppermute(piece.astype(BF16), 'gx', pairs))  13 us
    ppermute x6, waiting for transfers between devices, last(): return (piece, lax.ppermute(piece.astype(BF16), 'gx', pairs))  12.1 us
  transfers between devices with their start and end apart: 27, of which 10 were waited for; matrix products, arithmetic and copies ran while one was open for 32% of the time, Pallas kernels for 0%

profile of v1, /device:TPU:0, one launch (start us, length us, event | category | flops | bytes accessed | tf_op | source)
XLA Modules:
  0.0 439.9 jit_solution(12417920781758947819)
XLA Ops:
  0.6 7.2 %fusion.40 = (bf16[4,32,3072]{2,1,0:T(8,128)(2,1)}, bf16[4,32,3072]{2,1,0:T(8,128)(2,1)}, bf16[4,32,3072]{2,1,0:T(8,128)(2,1)S(1)}, bf16[4,32,3072]{2,1,0:T(8,128)(2,1)}) fusion(bf16[4,128,3072]{2,1,0:T(8,128)(2,1)} %bitcast.183, bf16[4,128,3072]{2,1,0:T(8,128)(2,1)} %bitcast.184), kind=kLoop, calls=%fused_computation.75 | loop fusion | flops 33030144 | bytes 9437184 | tf_op jit(solution)/shard_map/convert_element_type | solution.py:22
  7.8 1.8 pad_maximum_fusion.2
  9.6 1.7 copy-done.6
  11.3 15.0 %fusion.27 = bf16[512,3072]{1,0:T(8,128)(2,1)} fusion(bf16[512,3072]{1,0:T(8,128)(2,1)S(1)} %bitcast.179, bf16[1,6144,3072]{2,1,0:T(8,128)(2,1)} %param.5), kind=kOutput, calls=%fused_computation.22 | convolution fusion | flops 9665249280 | bytes 25165824 | tf_op jit(solution)/shard_map/dot_general | solution.py:37
  26.3 2.8 dynamic-slice_bitcast_fusion.1
  29.5 3.6 collective-permute-start.14
  33.1 15.1 %fusion.30 = bf16[512,3072]{1,0:T(8,128)(2,1)} fusion(bf16[512,3072]{1,0:T(8,128)(2,1)S(1)} %bitcast.181, bf16[1,6144,3072]{2,1,0:T(8,128)(2,1)} %param.5), kind=kOutput, calls=%fused_computation.23 | convolution fusion | flops 9665249280 | bytes 25165824 | tf_op jit(solution)/shard_map/dot_general | solution.py:37
  48.2 2.7 dynamic-slice_bitcast_fusion
  51.4 2.6 collective-permute-start.6
  54.0 48.0 %collective-permute-done.14 = bf16[128,3072]{1,0:T(8,128)(2,1)S(1)} collective-permute-done((bf16[128,3072]{1,0:T(8,128)(2,1)S(1)}, bf16[128,3072]{1,0:T(8,128)(2,1)S(1)}, u32[]{:S(2)}, u32[]{:S(2)}) %collective-permute-start.14) | collective-permute-done | bytes 786464 | tf_op jit(solution)/shard_map/ppermute | solution.py:27
  102.1 18.3 %fusion.21 = bf16[128,6144]{1,0:T(8,128)(2,1)S(1)} fusion(bf16[128,3072]{1,0:T(8,128)(2,1)S(1)} %collective-permute-done.14, bf16[1,6144,3072]{2,1,0:T(8,128)(2,1)} %param.5), kind=kOutput, calls=%fused_computation.18 | convolution fusion | flops 4832624640 | bytes 40108032 | tf_op jit(solution)/shard_map/dot_general | solution.py:37
  120.4 15.4 %collective-permute-done.18 = bf16[128,3072]{1,0:T(8,128)(2,1)S(1)} collective-permute-done((bf16[128,3072]{1,0:T(8,128)(2,1)}, bf16[128,3072]{1,0:T(8,128)(2,1)S(1)}, u32[]{:S(2)}, u32[]{:S(2)}) %collective-permute-start.18) | collective-permute-done | bytes 786464 | tf_op jit(solution)/shard_map/ppermute | solution.py:27
  137.3 17.8 %fusion.24 = bf16[128,6144]{1,0:T(8,128)(2,1)S(1)} fusion(bf16[128,3072]{1,0:T(8,128)(2,1)} %copy-done.5, bf16[1,6144,3072]{2,1,0:T(8,128)(2,1)} %param.5), kind=kOutput, calls=%fused_computation.19 | convolution fusion | flops 4832624640 | bytes 40108032 | tf_op jit(solution)/shard_map/dot_general | solution.py:37
  156.2 17.8 %fusion.15 = bf16[128,6144]{1,0:T(8,128)(2,1)S(1)} fusion(bf16[128,3072]{1,0:T(8,128)(2,1)} %collective-permute-done.6, bf16[1,6144,3072]{2,1,0:T(8,128)(2,1)} %param.5), kind=kOutput, calls=%fused_computation.16 | convolution fusion | flops 4832624640 | bytes 40108032 | tf_op jit(solution)/shard_map/dot_general | solution.py:37
  175.5 18.0 %fusion.18 = bf16[128,6144]{1,0:T(8,128)(2,1)S(1)} fusion(bf16[128,3072]{1,0:T(8,128)(2,1)} %collective-permute-done.10, bf16[1,6144,3072]{2,1,0:T(8,128)(2,1)} %param.5), kind=kOutput, calls=%fused_computation.17 | convolution fusion | flops 4832624640 | bytes 40108032 | tf_op jit(solution)/shard_map/dot_general | solution.py:37
  193.6 3.2 pad_maximum_fusion.5
  197.0 1.7 copy-done.9
  198.6 1.9 convert_add_fusion.5
  200.8 1.2 copy-done.3
  202.0 1.3 convert_add_fusion.7
  203.3 1.6 collective-permute-start.1
  204.9 1.9 convert_add_fusion.4
  208.2 1.3 convert_add_fusion.6
  210.8 1.3 collective-permute-start.20
  213.1 1.6 broadcast_select_fusion
  214.8 34.3 %collective-permute-done.16 = bf16[32,6144]{1,0:T(8,128)(2,1)S(1)} collective-permute-done((bf16[32,6144]{1,0:T(8,128)(2,1)S(1)}, bf16[32,6144]{1,0:T(8,128)(2,1)S(1)}, u32[]{:S(2)}, u32[]{:S(2)}) %collective-permute-start.16) | collective-permute-done | bytes 393248 | tf_op jit(solution)/shard_map/ppermute | solution.py:27
  249.1 1.5 collective-permute-start.12
  250.7 6.8 %collective-permute-done.20 = bf16[32,6144]{1,0:T(8,128)(2,1)S(1)} collective-permute-done((bf16[32,6144]{1,0:T(8,128)(2,1)S(1)}, bf16[32,6144]{1,0:T(8,128)(2,1)S(1)}, u32[]{:S(2)}, u32[]{:S(2)}) %collective-permute-start.20) | collective-permute-done | bytes 393248 | tf_op jit(solution)/shard_map/ppermute | solution.py:27
  257.5 1.5 collective-permute-start.23
  259.1 6.8 %collective-permute-done.8 = bf16[32,6144]{1,0:T(8,128)(2,1)S(1)} collective-permute-done((bf16[32,6144]{1,0:T(8,128)(2,1)S(1)}, bf16[32,6144]{1,0:T(8,128)(2,1)S(1)}, u32[]{:S(2)}, u32[]{:S(2)}) %collective-permute-start.8) | collective-permute-done | bytes 393248 | tf_op jit(solution)/shard_map/ppermute | solution.py:27
  265.9 1.5 collective-permute-start.25
  267.5 6.8 %collective-permute-done.12 = bf16[32,6144]{1,0:T(8,128)(2,1)S(1)} collective-permute-done((bf16[32,6144]{1,0:T(8,128)(2,1)S(1)}, bf16[32,6144]{1,0:T(8,128)(2,1)S(1)}, u32[]{:S(2)}, u32[]{:S(2)}) %collective-permute-start.12) | collective-permute-done | bytes 393248 | tf_op jit(solution)/shard_map/ppermute | solution.py:27
  274.3 3.2 collective-permute-start.17
  277.7 1.3 collective-permute-start.21
  279.3 1.3 collective-permute-start.9
  280.8 27.2 %collective-permute-done.23 = bf16[128,6144]{1,0:T(8,128)(2,1)S(1)} collective-permute-done((bf16[128,6144]{1,0:T(8,128)(2,1)S(1)}, bf16[128,6144]{1,0:T(8,128)(2,1)S(1)}, u32[]{:S(2)}, u32[]{:S(2)}) %collective-permute-start.23) | collective-permute-done | bytes 1572896 | tf_op jit(solution)/shard_map/ppermute | solution.py:27
  308.0 1.3 collective-permute-start.4
  309.6 31.3 %collective-permute-done.25 = bf16[128,6144]{1,0:T(8,128)(2,1)S(1)} collective-permute-done((bf16[128,6144]{1,0:T(8,128)(2,1)S(1)}, bf16[128,6144]{1,0:T(8,128)(2,1)S(1)}, u32[]{:S(2)}, u32[]{:S(2)}) %collective-permute-start.25) | collective-permute-done | bytes 1572896 | tf_op jit(solution)/shard_map/ppermute | solution.py:27
  340.8 1.3 collective-permute-start.5
  342.6 1.9 pad_maximum_fusion.4
  344.5 4.6 %collective-permute-start.13 = (bf16[32,6144]{1,0:T(8,128)(2,1)S(1)}, bf16[32,6144]{1,0:T(8,128)(2,1)S(1)}, u32[]{:S(2)}, u32[]{:S(2)}) collective-permute-start(bf16[32,6144]{1,0:T(8,128)(2,1)S(1)} %fusion.87), channel_id=1, source_target_pairs={{0,4},{1,5},{2,6},{3,7},{12,8},{13,9},{14,10},{15,11},{16,20},{17,... | collective-permute-start | bytes 1179656 | tf_op jit(solution)/shard_map/ppermute | solution.py:109
  349.2 12.1 %collective-permute-done.5 = bf16[128,3072]{1,0:T(8,128)(2,1)S(1)} collective-permute-done((bf16[128,3072]{1,0:T(8,128)(2,1)S(1)}, bf16[128,3072]{1,0:T(8,128)(2,1)S(1)}, u32[]{:S(2)}, u32[]{:S(2)}) %collective-permute-start.5) | collective-permute-done | bytes 786464 | tf_op jit(solution)/shard_map/ppermute | solution.py:109
  362.9 1.3 maximum_bitcast_fusion
  364.1 6.0 %collective-permute-done.24 = bf16[2,128,6144]{2,1,0:T(8,128)(2,1)S(1)} collective-permute-done((bf16[2,128,6144]{2,1,0:T(8,128)(2,1)S(1)}, bf16[2,128,6144]{2,1,0:T(8,128)(2,1)S(1)}, u32[]{:S(2)}, u32[]{:S(2)}) %collective-permute-start.24) | collective-permute-done | bytes 3145760 | tf_op jit(solution)/shard_map/ppermute | solution.py:27
  370.8 3.2 pad_maximum_fusion
  374.0 28.2 %fusion.96 = bf16[6144,3072]{1,0:T(8,128)(2,1)} fusion(bf16[512,6144]{1,0:T(8,128)(2,1)} %bitcast.174, bf16[512,3072]{1,0:T(8,128)(2,1)} %bitcast.180), kind=kOutput, calls=%fused_computation.163 | convolution fusion | flops 19327352832 | bytes 47185920 | tf_op jit(solution)/shard_map/dot_general | solution.py:41
  402.2 2.1 select_bitcast_fusion.1
  405.7 33.7 %fusion = bf16[1,6144,3072]{2,1,0:T(8,128)(2,1)} fusion(bf16[6144,3072]{1,0:T(8,128)(2,1)} %fusion.96, bf16[512,6144]{1,0:T(8,128)(2,1)S(1)} %bitcast.175, bf16[512,3072]{1,0:T(8,128)(2,1)} %bitcast.182), kind=kOutput, calls=%fused_computation.1 | convolution fusion | flops 19383975936 | bytes 84934656 | tf_op jit(solution)/shard_map/dot_general | solution.py:41
  (78 shorter events, 14.1 us)
Async XLA Ops:
  9.6 1.7 copy-start.6
  26.3 6.8 %copy-start.7 = (bf16[4,128,3072]{2,1,0:T(8,128)(2,1)S(1)}, bf16[4,128,3072]{2,1,0:T(8,128)(2,1)}, u32[]{:S(2)}) copy-start(bf16[4,128,3072]{2,1,0:T(8,128)(2,1)} %copy-done.6) | copy-start | bytes 9437188
  29.1 167.8 %collective-permute-start = (bf16[2,128,3072]{2,1,0:T(8,128)(2,1)}, bf16[2,128,3072]{2,1,0:T(8,128)(2,1)}, u32[]{:S(2)}, u32[]{:S(2)}) collective-permute-start(bf16[2,128,3072]{2,1,0:T(8,128)(2,1)} %dynamic-slice_bitcast_fusion.1), channel_id=1, source_target_pairs={{0,1},{1,0},{2,3},{3,2},{4,5},{5,4},{6,7},{7,6},{8,9},{9,8},{10,11... | collective-permute-start | bytes 4718600 | tf_op jit(solution)/shard_map/ppermute | solution.py:27
  29.5 72.5 %collective-permute-start.14 = (bf16[128,3072]{1,0:T(8,128)(2,1)S(1)}, bf16[128,3072]{1,0:T(8,128)(2,1)S(1)}, u32[]{:S(2)}, u32[]{:S(2)}) collective-permute-start(bf16[128,3072]{1,0:T(8,128)(2,1)S(1)} %bitcast.178), channel_id=1, source_target_pairs={{0,8},{1,9},{2,10},{3,11},{4,12},{5,13},{6,14},{7,15},{8,0},{9,1},... | collective-permute-start | bytes 2359304 | tf_op jit(solution)/shard_map/ppermute | solution.py:27
  50.9 152.4 %collective-permute-start.2 = (bf16[2,128,3072]{2,1,0:T(8,128)(2,1)}, bf16[2,128,3072]{2,1,0:T(8,128)(2,1)}, u32[]{:S(2)}, u32[]{:S(2)}) collective-permute-start(bf16[2,128,3072]{2,1,0:T(8,128)(2,1)} %dynamic-slice_bitcast_fusion), channel_id=1, source_target_pairs={{0,1},{1,0},{2,3},{3,2},{4,5},{5,4},{6,7},{7,6},{8,9},{9,8},{10,11... | collective-permute-start | bytes 4718600 | tf_op jit(solution)/shard_map/ppermute | solution.py:27
  51.1 84.7 %collective-permute-start.18 = (bf16[128,3072]{1,0:T(8,128)(2,1)}, bf16[128,3072]{1,0:T(8,128)(2,1)S(1)}, u32[]{:S(2)}, u32[]{:S(2)}) collective-permute-start(bf16[128,3072]{1,0:T(8,128)(2,1)} %bitcast.34), channel_id=1, source_target_pairs={{0,8},{1,9},{2,10},{3,11},{4,12},{5,13},{6,14},{7,15},{8,0},{9,1},... | collective-permute-start | bytes 2359304 | tf_op jit(solution)/shard_map/ppermute | solution.py:27
  51.4 104.8 %collective-permute-start.6 = (bf16[128,3072]{1,0:T(8,128)(2,1)}, bf16[128,3072]{1,0:T(8,128)(2,1)}, u32[]{:S(2)}, u32[]{:S(2)}) collective-permute-start(bf16[128,3072]{1,0:T(8,128)(2,1)} %bitcast.15), channel_id=1, source_target_pairs={{0,8},{1,9},{2,10},{3,11},{4,12},{5,13},{6,14},{7,15},{8,0},{9,1},... | collective-permute-start | bytes 2359304 | tf_op jit(solution)/shard_map/ppermute | solution.py:27
  102.1 18.3 %copy-start.4 = (bf16[128,3072]{1,0:T(8,128)(2,1)}, bf16[128,3072]{1,0:T(8,128)(2,1)S(1)}, u32[]{:S(2)}) copy-start(bf16[128,3072]{1,0:T(8,128)(2,1)S(1)} %collective-permute-done.14) | copy-start | bytes 2359300
  102.1 73.0 %collective-permute-start.10 = (bf16[128,3072]{1,0:T(8,128)(2,1)}, bf16[128,3072]{1,0:T(8,128)(2,1)}, u32[]{:S(2)}, u32[]{:S(2)}) collective-permute-start(bf16[128,3072]{1,0:T(8,128)(2,1)} %bitcast.22), channel_id=1, source_target_pairs={{0,8},{1,9},{2,10},{3,11},{4,12},{5,13},{6,14},{7,15},{8,0},{9,1},... | collective-permute-start | bytes 2359304 | tf_op jit(solution)/shard_map/ppermute | solution.py:27
  120.4 34.8 %copy-start.2 = (bf16[128,6144]{1,0:T(8,128)(2,1)}, bf16[128,6144]{1,0:T(8,128)(2,1)S(1)}, u32[]{:S(2)}) copy-start(bf16[128,6144]{1,0:T(8,128)(2,1)S(1)} %fusion.21) | copy-start | bytes 4718596
  135.8 0.9 copy-start.5
  136.7 75.6 %collective-permute-start.22 = (bf16[128,6144]{1,0:T(8,128)(2,1)}, bf16[128,6144]{1,0:T(8,128)(2,1)}, u32[]{:S(2)}, u32[]{:S(2)}) collective-permute-start(bf16[128,6144]{1,0:T(8,128)(2,1)} %bitcast.189), channel_id=1, source_target_pairs={{0,4},{1,5},{2,6},{3,7},{4,0},{5,1},{6,2},{7,3},{8,12},{9,13},{10,... | collective-permute-start | bytes 4718600 | tf_op jit(solution)/shard_map/ppermute | solution.py:27
  155.2 18.9 %copy-start = (bf16[128,6144]{1,0:T(8,128)(2,1)}, bf16[128,6144]{1,0:T(8,128)(2,1)S(1)}, u32[]{:S(2)}) copy-start(bf16[128,6144]{1,0:T(8,128)(2,1)S(1)} %fusion.24) | copy-start | bytes 4718596
  156.2 44.5 %collective-permute-start.15 = (bf16[2,32,6144]{2,1,0:T(8,128)(2,1)}, bf16[2,32,6144]{2,1,0:T(8,128)(2,1)}, u32[]{:S(2)}, u32[]{:S(2)}) collective-permute-start(bf16[2,32,6144]{2,1,0:T(8,128)(2,1)} %dynamic-slice_bitcast_fusion.3), channel_id=1, source_target_pairs={{0,1},{1,0},{2,3},{3,2},{4,5},{5,4},{6,7},{7,6},{8,9},{9,8},{10,11... | collective-permute-start | bytes 2359304 | tf_op jit(solution)/shard_map/ppermute | solution.py:27
  175.0 31.9 %collective-permute-start.19 = (bf16[2,32,6144]{2,1,0:T(8,128)(2,1)}, bf16[2,32,6144]{2,1,0:T(8,128)(2,1)}, u32[]{:S(2)}, u32[]{:S(2)}) collective-permute-start(bf16[2,32,6144]{2,1,0:T(8,128)(2,1)} %dynamic-slice_bitcast_fusion.2), channel_id=1, source_target_pairs={{0,1},{1,0},{2,3},{3,2},{4,5},{5,4},{6,7},{7,6},{8,9},{9,8},{10,11... | collective-permute-start | bytes 2359304 | tf_op jit(solution)/shard_map/ppermute | solution.py:27
  196.8 1.9 copy-start.9
  196.9 12.7 %collective-permute-start.7 = (bf16[2,32,6144]{2,1,0:T(8,128)(2,1)S(1)}, bf16[2,32,6144]{2,1,0:T(8,128)(2,1)S(1)}, u32[]{:S(2)}, u32[]{:S(2)}) collective-permute-start(bf16[2,32,6144]{2,1,0:T(8,128)(2,1)S(1)} %dynamic-slice_bitcast_fusion.5), channel_id=1, source_target_pairs={{0,1},{1,0},{2,3},{3,2},{4,5},{5,4},{6,7},{7,6},{8,9},{9,8},{10,11... | collective-permute-start | bytes 2359304 | tf_op jit(solution)/shard_map/ppermute | solution.py:27
  200.6 1.4 copy-start.3
  200.7 4.2 copy-start.8
  200.7 10.1 %collective-permute-start.11 = (bf16[2,32,6144]{2,1,0:T(8,128)(2,1)S(1)}, bf16[2,32,6144]{2,1,0:T(8,128)(2,1)S(1)}, u32[]{:S(2)}, u32[]{:S(2)}) collective-permute-start(bf16[2,32,6144]{2,1,0:T(8,128)(2,1)S(1)} %dynamic-slice_bitcast_fusion.4), channel_id=1, source_target_pairs={{0,1},{1,0},{2,3},{3,2},{4,5},{5,4},{6,7},{7,6},{8,9},{9,8},{10,11... | collective-permute-start | bytes 2359304 | tf_op jit(solution)/shard_map/ppermute | solution.py:27
  203.3 74.4 %collective-permute-start.1 = (bf16[128,3072]{1,0:T(8,128)(2,1)S(1)}, bf16[128,3072]{1,0:T(8,128)(2,1)S(1)}, u32[]{:S(2)}, u32[]{:S(2)}) collective-permute-start(bf16[128,3072]{1,0:T(8,128)(2,1)S(1)} %fusion.69), channel_id=1, source_target_pairs={{0,2},{1,3},{2,0},{3,1},{4,6},{5,7},{6,4},{7,5},{8,10},{9,11},{10,... | collective-permute-start | bytes 2359304 | tf_op jit(solution)/shard_map/ppermute | solution.py:27
  206.8 1.4 copy-start.1
  207.0 72.3 %collective-permute-start.3 = (bf16[128,3072]{1,0:T(8,128)(2,1)S(1)}, bf16[128,3072]{1,0:T(8,128)(2,1)S(1)}, u32[]{:S(2)}, u32[]{:S(2)}) collective-permute-start(bf16[128,3072]{1,0:T(8,128)(2,1)S(1)} %fusion.70), channel_id=1, source_target_pairs={{0,2},{1,3},{2,0},{3,1},{4,6},{5,7},{6,4},{7,5},{8,10},{9,11},{10,... | collective-permute-start | bytes 2359304 | tf_op jit(solution)/shard_map/ppermute | solution.py:27
  209.6 39.5 %collective-permute-start.16 = (bf16[32,6144]{1,0:T(8,128)(2,1)S(1)}, bf16[32,6144]{1,0:T(8,128)(2,1)S(1)}, u32[]{:S(2)}, u32[]{:S(2)}) collective-permute-start(bf16[32,6144]{1,0:T(8,128)(2,1)S(1)} %fusion.92), channel_id=1, source_target_pairs={{0,2},{1,3},{2,0},{3,1},{4,6},{5,7},{6,4},{7,5},{8,10},{9,11},{10,... | collective-permute-start | bytes 1179656 | tf_op jit(solution)/shard_map/ppermute | solution.py:27
  210.8 2.4 copy-start.10
  210.8 46.7 %collective-permute-start.20 = (bf16[32,6144]{1,0:T(8,128)(2,1)S(1)}, bf16[32,6144]{1,0:T(8,128)(2,1)S(1)}, u32[]{:S(2)}, u32[]{:S(2)}) collective-permute-start(bf16[32,6144]{1,0:T(8,128)(2,1)S(1)} %fusion.93), channel_id=1, source_target_pairs={{0,2},{1,3},{2,0},{3,1},{4,6},{5,7},{6,4},{7,5},{8,10},{9,11},{10,... | collective-permute-start | bytes 1179656 | tf_op jit(solution)/shard_map/ppermute | solution.py:27
  212.2 53.7 %collective-permute-start.8 = (bf16[32,6144]{1,0:T(8,128)(2,1)S(1)}, bf16[32,6144]{1,0:T(8,128)(2,1)S(1)}, u32[]{:S(2)}, u32[]{:S(2)}) collective-permute-start(bf16[32,6144]{1,0:T(8,128)(2,1)S(1)} %fusion.90), channel_id=1, source_target_pairs={{0,2},{1,3},{2,0},{3,1},{4,6},{5,7},{6,4},{7,5},{8,10},{9,11},{10,... | collective-permute-start | bytes 1179656 | tf_op jit(solution)/shard_map/ppermute | solution.py:27
  249.1 25.3 %collective-permute-start.12 = (bf16[32,6144]{1,0:T(8,128)(2,1)S(1)}, bf16[32,6144]{1,0:T(8,128)(2,1)S(1)}, u32[]{:S(2)}, u32[]{:S(2)}) collective-permute-start(bf16[32,6144]{1,0:T(8,128)(2,1)S(1)} %fusion.91), channel_id=1, source_target_pairs={{0,2},{1,3},{2,0},{3,1},{4,6},{5,7},{6,4},{7,5},{8,10},{9,11},{10,... | collective-permute-start | bytes 1179656 | tf_op jit(solution)/shard_map/ppermute | solution.py:27
  257.5 50.6 %collective-permute-start.23 = (bf16[128,6144]{1,0:T(8,128)(2,1)S(1)}, bf16[128,6144]{1,0:T(8,128)(2,1)S(1)}, u32[]{:S(2)}, u32[]{:S(2)}) collective-permute-start(bf16[128,6144]{1,0:T(8,128)(2,1)S(1)} %get-tuple-element.21), channel_id=1, source_target_pairs={{0,2},{1,3},{2,0},{3,1},{4,6},{5,7},{6,4},{7,5},{8,10},{9,11},{10,... | collective-permute-start | bytes 4718600 | tf_op jit(solution)/shard_map/ppermute | solution.py:27
  265.9 74.9 %collective-permute-start.25 = (bf16[128,6144]{1,0:T(8,128)(2,1)S(1)}, bf16[128,6144]{1,0:T(8,128)(2,1)S(1)}, u32[]{:S(2)}, u32[]{:S(2)}) collective-permute-start(bf16[128,6144]{1,0:T(8,128)(2,1)S(1)} %get-tuple-element.20), channel_id=1, source_target_pairs={{0,2},{1,3},{2,0},{3,1},{4,6},{5,7},{6,4},{7,5},{8,10},{9,11},{10,... | collective-permute-start | bytes 4718600 | tf_op jit(solution)/shard_map/ppermute | solution.py:27
  274.3 87.0 %collective-permute-start.17 = (bf16[32,6144]{1,0:T(8,128)(2,1)S(1)}, bf16[32,6144]{1,0:T(8,128)(2,1)S(1)}, u32[]{:S(2)}, u32[]{:S(2)}) collective-permute-start(bf16[32,6144]{1,0:T(8,128)(2,1)S(1)} %fusion.88), channel_id=1, source_target_pairs={{0,4},{1,5},{2,6},{3,7},{12,8},{13,9},{14,10},{15,11},{16,20},{17,... | collective-permute-start | bytes 1179656 | tf_op jit(solution)/shard_map/ppermute | solution.py:109
  277.7 84.3 %collective-permute-start.21 = (bf16[32,6144]{1,0:T(8,128)(2,1)S(1)}, bf16[32,6144]{1,0:T(8,128)(2,1)S(1)}, u32[]{:S(2)}, u32[]{:S(2)}) collective-permute-start(bf16[32,6144]{1,0:T(8,128)(2,1)S(1)} %fusion.89), channel_id=1, source_target_pairs={{0,4},{1,5},{2,6},{3,7},{12,8},{13,9},{14,10},{15,11},{16,20},{17,... | collective-permute-start | bytes 1179656 | tf_op jit(solution)/shard_map/ppermute | solution.py:109
  279.3 83.1 %collective-permute-start.9 = (bf16[32,6144]{1,0:T(8,128)(2,1)S(1)}, bf16[32,6144]{1,0:T(8,128)(2,1)S(1)}, u32[]{:S(2)}, u32[]{:S(2)}) collective-permute-start(bf16[32,6144]{1,0:T(8,128)(2,1)S(1)} %fusion.86), channel_id=1, source_target_pairs={{0,4},{1,5},{2,6},{3,7},{12,8},{13,9},{14,10},{15,11},{16,20},{17,... | collective-permute-start | bytes 1179656 | tf_op jit(solution)/shard_map/ppermute | solution.py:109
  308.0 36.5 %collective-permute-start.4 = (bf16[128,3072]{1,0:T(8,128)(2,1)S(1)}, bf16[128,3072]{1,0:T(8,128)(2,1)S(1)}, u32[]{:S(2)}, u32[]{:S(2)}) collective-permute-start(bf16[128,3072]{1,0:T(8,128)(2,1)S(1)} %get-tuple-element.4), channel_id=1, source_target_pairs={{4,0},{5,1},{6,2},{7,3},{8,12},{9,13},{10,14},{11,15},{20,16},{21,... | collective-permute-start | bytes 2359304 | tf_op jit(solution)/shard_map/ppermute | solution.py:109
  340.8 20.5 %collective-permute-start.5 = (bf16[128,3072]{1,0:T(8,128)(2,1)S(1)}, bf16[128,3072]{1,0:T(8,128)(2,1)S(1)}, u32[]{:S(2)}, u32[]{:S(2)}) collective-permute-start(bf16[128,3072]{1,0:T(8,128)(2,1)S(1)} %get-tuple-element.2), channel_id=1, source_target_pairs={{4,0},{5,1},{6,2},{7,3},{8,12},{9,13},{10,14},{11,15},{20,16},{21,... | collective-permute-start | bytes 2359304 | tf_op jit(solution)/shard_map/ppermute | solution.py:109
  344.5 17.9 %collective-permute-start.13 = (bf16[32,6144]{1,0:T(8,128)(2,1)S(1)}, bf16[32,6144]{1,0:T(8,128)(2,1)S(1)}, u32[]{:S(2)}, u32[]{:S(2)}) collective-permute-start(bf16[32,6144]{1,0:T(8,128)(2,1)S(1)} %fusion.87), channel_id=1, source_target_pairs={{0,4},{1,5},{2,6},{3,7},{12,8},{13,9},{14,10},{15,11},{16,20},{17,... | collective-permute-start | bytes 1179656 | tf_op jit(solution)/shard_map/ppermute | solution.py:109
  361.3 8.8 %collective-permute-start.24 = (bf16[2,128,6144]{2,1,0:T(8,128)(2,1)S(1)}, bf16[2,128,6144]{2,1,0:T(8,128)(2,1)S(1)}, u32[]{:S(2)}, u32[]{:S(2)}) collective-permute-start(bf16[2,128,6144]{2,1,0:T(8,128)(2,1)S(1)} %pad_maximum_fusion.3), channel_id=1, source_target_pairs={{0,1},{1,0},{2,3},{3,2},{4,5},{5,4},{6,7},{7,6},{8,9},{9,8},{10,11... | collective-permute-start | bytes 9437192 | tf_op jit(solution)/shard_map/ppermute | solution.py:27
  361.4 40.8 %collective-permute-start.26 = (bf16[2,128,6144]{2,1,0:T(8,128)(2,1)}, bf16[2,128,6144]{2,1,0:T(8,128)(2,1)}, u32[]{:S(2)}, u32[]{:S(2)}) collective-permute-start(bf16[2,128,6144]{2,1,0:T(8,128)(2,1)} %pad_maximum_fusion.4), channel_id=1, source_target_pairs={{0,1},{1,0},{2,3},{3,2},{4,5},{5,4},{6,7},{7,6},{8,9},{9,8},{10,11... | collective-permute-start | bytes 9437192 | tf_op jit(solution)/shard_map/ppermute | solution.py:27

commit v2 on v1

--- a/solution.py
+++ b/solution.py
@@ -6,7 +6,8 @@
 from jax.sharding import PartitionSpec as P
 
 GC = 8
-CHUNKS = 4
+PIECES = (6, 4, 4, 2)
+GROUPS = ((0, 1), (2, 3))
 F32 = jnp.float32
 BF16 = jnp.bfloat16
 
@@ -68,70 +69,98 @@
     return part.astype(BF16), weight_grad
 
 
+def after(array, *others):
+    return lax.optimization_barrier((array, *others))[0]
+
+
 def two_rows(index, x, w, preact, out_grad):
     row, z, y, core = index // GC, index // 4 % 2, index // 2 % 2, index % 2
     tokens, width = x.shape
     hidden = w.shape[1]
-    step = tokens // CHUNKS
+    unit = tokens // sum(PIECES)
     mine = z == row
-
-    g4, p4 = out_grad.reshape(4, tokens, hidden), preact.reshape(4, tokens, hidden)
-    dy_own, dy_other = [], []
-    for q in range(CHUNKS):
-        part = slice(q * step, (q + 1) * step)
-        dy_own.append(gelu_slope(g4[:, part], p4[:, part]).reshape(4 * step, hidden))
-        dy_other.append(swap(dy_own[-1], GC))
-
-    partner = swap(x, 4)
-    x_own, x_other = jnp.where(mine, x, partner), jnp.where(mine, partner, x)
-
-    def spread(piece):
-        piece = join(y, piece[None], swap(piece, 2)[None], 0)
-        piece = join(core, piece[:, None], swap(piece, 1)[:, None], 1)
-        return piece.reshape(4 * tokens, width)
-
-    def order(chunks):
-        return jnp.concatenate([c.reshape(4, step, hidden) for c in chunks], 1).reshape(
-            4 * tokens, hidden
-        )
-
-    def reduce(part):
-        part = part.reshape(2, 2, -1, part.shape[-1])
-        part = take(part, core, 1).astype(F32) + swap(take(part, 1 - core, 1), 1).astype(F32)
-        sent = take(part, 1 - y, 0).astype(BF16)
-        return take(part, y, 0) + swap(sent, 2).astype(F32)
-
     size = lax.axis_size("gx")
     to_own = [(i, i ^ 4) for i in range(size) if i // 4 % 2 != i // GC]
     to_other = [(i, i ^ 4) for i in range(size) if i // 4 % 2 == i // GC]
 
+    def order(pieces):
+        pieces = [piece.reshape(4, -1, hidden) for piece in pieces]
+        return jnp.concatenate(pieces, 1).reshape(-1, hidden)
+
+    def reduce_core(part):
+        part = part.reshape(2, 2, -1, part.shape[-1])
+        return take(part, core, 1).astype(F32) + swap(take(part, 1 - core, 1), 1).astype(F32)
+
+    def reduce_y(part, *others):
+        received = swap(take(part, 1 - y, 0).astype(BF16), 2)
+        return take(part, y, 0) + after(received, *others).astype(F32)
+
     def last(piece, pairs):
-        return piece, lax.ppermute(piece.astype(BF16), "gx", pairs)
+        return lax.ppermute(piece.astype(BF16), "gx", pairs)
 
-    own_rows = order(dy_own)
-    half = width // 2
-    own_sum, own_recv = [], []
-    for h in range(2):
-        part = times_wt(own_rows, w[h * half : (h + 1) * half]).astype(BF16)
-        kept, recv = last(reduce(part), to_own)
-        own_sum.append(kept)
-        own_recv.append(recv)
-    own_sum, own_recv = jnp.concatenate(own_sum, 1), jnp.concatenate(own_recv, 1)
+    top, bottom = x[: tokens // 2], x[tokens // 2 :]
+    top_z, top_y = swap(top, 4), swap(top, 2)
+    own_rows = after(gelu_slope(out_grad, preact))
+    split = own_rows.reshape(4, tokens, hidden)
+    dy = []
 
-    dw_own = xt_times(spread(x_own), own_rows).astype(BF16)
+    def send_piece(*others):
+        low, high = (sum(PIECES[: len(dy) + more]) * unit for more in (0, 1))
+        sent = split[:, low:high].reshape(-1, hidden)
+        dy.append(swap(after(sent, *dy[-1:], *others), GC))
 
-    outs = []
-    for q in range(CHUNKS):
-        kept, recv = last(reduce(times_wt(dy_other[q], w).astype(BF16)), to_other)
-        part = slice(q * step, (q + 1) * step)
+    send_piece()
+
+    own_rows, top_z, top_y, bottom = lax.optimization_barrier((own_rows, top_z, top_y, bottom))
+    bottom_z, bottom_y = swap(bottom, 4), swap(bottom, 2)
+    own = times_wt(own_rows, w).astype(BF16)
+    own, bottom_z, bottom_y, dy[0] = lax.optimization_barrier((own, bottom_z, bottom_y, dy[0]))
+    send_piece()
+    x_z = jnp.concatenate([top_z, bottom_z], 0)
+    x_y = jnp.concatenate([top_y, bottom_y], 0)
+    x_zy = swap(x_z, 2)
+    own_core = reduce_core(own)
+
+    dy[1], x_zy, own_core = lax.optimization_barrier((dy[1], x_zy, own_core))
+    send_piece()
+
+    def finish(near, far):
+        piece = join(y, near[None], far[None], 0)
+        piece = join(core, piece[:, None], swap(piece, 1)[:, None], 1)
+        return piece.reshape(4 * tokens, width)
+
+    def partial_of(group, *others):
+        rows = after(order([dy[q] for q in group]), *others)
+        return times_wt(rows, w).astype(BF16)
+
+    own_x = finish(jnp.where(mine, x, x_z), jnp.where(mine, x_y, x_zy))
+    rest_x = finish(jnp.where(mine, x_z, x), jnp.where(mine, x_zy, x_y))
+    other, dy[2] = lax.optimization_barrier((partial_of(GROUPS[0]), dy[2]))
+    send_piece()
+    own_sum = reduce_y(own_core, other)
+    core_sum = [reduce_core(other)]
+    own_x = after(own_x, core_sum[0], own_sum)
+    dw_own = xt_times(own_x, own_rows).astype(BF16)
+    kept = [reduce_y(core_sum[0], dw_own)]
+    core_sum.append(reduce_core(partial_of(GROUPS[1], dw_own, rest_x, kept[0])))
+    own_recv, recv = last(own_sum, to_own), [last(kept[0], to_other)]
+
+    all_other = after(order(dy), core_sum[1])
+    weight_grad = (dw_own.astype(F32) + xt_times(rest_x, all_other)).astype(BF16)
+    kept.append(reduce_y(core_sum[1], weight_grad))
+    recv.append(last(kept[1], to_other))
+    own_recv, weight_grad, recv[0] = lax.optimization_barrier((own_recv, weight_grad, recv[0]))
+    outs, start = [], 0
+    for q in range(len(GROUPS)):
+        part = slice(start, start + kept[q].shape[0])
+        start = part.stop
         outs.append(
             jnp.where(
                 mine,
                 own_sum[part] + own_recv[part].astype(F32),
-                kept + recv.astype(F32),
+                kept[q] + recv[q].astype(F32),
             ).astype(BF16)
         )
-    weight_grad = (dw_own.astype(F32) + xt_times(spread(x_other), order(dy_other))).astype(BF16)
     return jnp.concatenate(outs, 0), weight_grad
 
 

time: 449 us -> 325 us (0.72); the launches traced: 440 us -> 325 us
  waiting for transfers between devices: 195 us -> 112 us
  matrix products: 164 us -> 129 us
  local copies, waits for them, and re-layouts: 15 us -> 22.6 us
  starting transfers between devices: 31.9 us -> 26.6 us
    ppermute x21 -> x17, waiting for transfers between devices: 183 us -> 101 us  [swap(): return lax.ppermute(array, 'gx', [(i, i ^ distance) for i in range(size)])]
    dot_general x6 -> x3, matrix products: 102 us -> 65.8 us  [times_wt(): lax.dot_general(rows, w, (((1,), (1,)), ((), ())), preferred_element_type...]
    convert_element_type x6 -> x3, other arithmetic: 0.75 us -> 6.66 us  [last(): return lax.ppermute(piece.astype(BF16), 'gx', pairs)]
    slice x0 -> x4, local copies, waits for them, and re-layouts: none -> 5.13 us  [the longest x1 2.8 us: two_rows(): top, bottom = (x[:tokens // 2], x[tokens // 2:])]
    add x6 -> x3, other arithmetic: 6.75 us -> 1.87 us  [reduce_core(): take(part, core, 1).astype(F32)]
    ppermute x6 -> x3, starting transfers between devices: 13 us -> 8.23 us  [last(): return lax.ppermute(piece.astype(BF16), 'gx', pairs)]
    ppermute x6 -> x3, waiting for transfers between devices: 12.1 us -> 10.9 us  [last(): return lax.ppermute(piece.astype(BF16), 'gx', pairs)]
    ppermute x21 -> x17, starting transfers between devices: 18.9 us -> 18.4 us  [swap(): return lax.ppermute(array, 'gx', [(i, i ^ distance) for i in range(size)])]
  transfers between devices with their start and end apart: 27 -> 20, of which waited for: 10 -> 7; matrix products, arithmetic and copies ran while one was open for 32% -> 47% of each run, Pallas kernels for 0% -> 0%
where the time goes in v2:
time: 325 us
  matrix products  129 us (40%)
  waiting for transfers between devices  112 us (34%)
  other arithmetic  33.8 us (10%)
  starting transfers between devices  26.6 us (8%)
  local copies, waits for them, and re-layouts  22.6 us (7%)
    ppermute x17, waiting for transfers between devices, swap(): return lax.ppermute(array, 'gx', [(i, i ^ distance) for i in range(size)])  101 us
    dot_general x3, matrix products, times_wt(): lax.dot_general(rows, w, (((1,), (1,)), ((), ())), preferred_element_type...  65.8 us
    dot_general x2, matrix products, xt_times(): lax.dot_general(x, dy, (((0,), (0,)), ((), ())), preferred_element_type=F32)  62.7 us
    ppermute x17, starting transfers between devices, swap(): return lax.ppermute(array, 'gx', [(i, i ^ distance) for i in range(size)])  18.4 us
    ppermute x3, waiting for transfers between devices, last(): return lax.ppermute(piece.astype(BF16), 'gx', pairs)  10.9 us
    ppermute x3, starting transfers between devices, last(): return lax.ppermute(piece.astype(BF16), 'gx', pairs)  8.23 us
    convert_element_type x3, other arithmetic, last(): return lax.ppermute(piece.astype(BF16), 'gx', pairs)  6.66 us
  transfers between devices with their start and end apart: 20, of which 7 were waited for; matrix products, arithmetic and copies ran while one was open for 47% of the time, Pallas kernels for 0%

profile of v2, /device:TPU:0, one launch (start us, length us, event | category | flops | bytes accessed | tf_op | source)
XLA Modules:
  0.0 324.7 jit_solution(9090974055044640185)
XLA Ops:
  0.6 2.8 slice_bitcast_fusion
  3.4 3.0 collective-permute-start
  6.5 1.5 collective-permute-start.1
  8.0 5.8 %fusion.22 = bf16[512,3072]{1,0:T(8,128)(2,1)S(1)} fusion(bf16[1,512,3072]{2,1,0:T(8,128)(2,1)S(1)} %copy-done.10, bf16[1,512,3072]{2,1,0:T(8,128)(2,1)} %param.6), kind=kLoop, calls=%fused_computation.25 | loop fusion | flops 33030144 | bytes 9437184 | tf_op jit(solution)/shard_map/convert_element_type | solution.py:23
  13.8 1.2 slice.49
  15.0 2.6 collective-permute-start.4
  17.7 15.1 %collective-permute-done = bf16[64,6144]{1,0:T(8,128)(2,1)} collective-permute-done((bf16[64,6144]{1,0:T(8,128)(2,1)}, bf16[64,6144]{1,0:T(8,128)(2,1)}, u32[]{:S(2)}, u32[]{:S(2)}) %collective-permute-start) | collective-permute-done | bytes 786464 | tf_op jit(solution)/shard_map/ppermute | solution.py:28
  32.8 2.7 collective-permute-start.3
  35.5 26.0 %fusion.6 = bf16[512,6144]{1,0:T(8,128)(2,1)} fusion(bf16[512,3072]{1,0:T(8,128)(2,1)S(1)} %fusion.22, bf16[1,6144,3072]{2,1,0:T(8,128)(2,1)} %param.5), kind=kOutput, calls=%fused_computation.15 | convolution fusion | flops 19330498560 | bytes 47185920 | tf_op jit(solution)/shard_map/dot_general | solution.py:38
  61.5 7.2 %collective-permute-done.4 = bf16[192,3072]{1,0:T(8,128)(2,1)} collective-permute-done((bf16[192,3072]{1,0:T(8,128)(2,1)}, bf16[192,3072]{1,0:T(8,128)(2,1)}, u32[]{:S(2)}, u32[]{:S(2)}) %collective-permute-start.4) | collective-permute-done | bytes 1179680 | tf_op jit(solution)/shard_map/ppermute | solution.py:28
  68.7 2.4 dynamic-slice_bitcast_fusion
  72.3 1.2 constant_dynamic-update-slice_fusion.1
  73.5 1.2 constant_dynamic-update-slice_fusion.3
  74.7 1.5 collective-permute-start.5
  76.2 1.2 constant_dynamic-update-slice_fusion
  77.4 1.6 collective-permute-start.6
  79.0 1.2 constant_dynamic-update-slice_fusion.2
  80.2 1.2 copy-done.6
  82.5 29.9 %collective-permute-done.5 = bf16[128,3072]{1,0:T(8,128)(2,1)S(1)} collective-permute-done((bf16[128,3072]{1,0:T(8,128)(2,1)S(1)}, bf16[128,3072]{1,0:T(8,128)(2,1)S(1)}, u32[]{:S(2)}, u32[]{:S(2)}) %collective-permute-start.5) | collective-permute-done | bytes 786464 | tf_op jit(solution)/shard_map/ppermute | solution.py:28
  112.4 1.6 collective-permute-done.6
  114.0 1.4 fusion.26
  115.4 1.5 collective-permute-start.8
  116.9 1.4 pad_maximum_fusion.5
  118.4 20.4 %fusion.9 = bf16[320,6144]{1,0:T(8,128)(2,1)} fusion(bf16[320,3072]{1,0:T(8,128)(2,1)S(1)} %bitcast.138, bf16[1,6144,3072]{2,1,0:T(8,128)(2,1)} %param.5), kind=kOutput, calls=%fused_computation.16 | convolution fusion | flops 12081561600 | bytes 43646976 | tf_op jit(solution)/shard_map/dot_general | solution.py:38
  138.8 1.2 collective-permute-start.9
  140.0 3.3 %select_bitcast_fusion.5 = (bf16[1,128,6144]{2,1,0:T(8,128)(2,1)S(1)}, bf16[1,128,6144]{2,1,0:T(8,128)(2,1)S(1)}, bf16[1,128,6144]{2,1,0:T(8,128)(2,1)S(1)}, bf16[1,128,6144]{2,1,0:T(8,128)(2,1)S(1)}) fusion(pred[]{:T(512)S(6)} %eq.21, bf16[128,6144]{1,0:T(8,128)(2,1)} %copy-done.14, bf16[128,6144]{1,0:T(8,128)(2,1)} %copy-done.6, pred[]{:T(512)S(6)} %eq.10, ...), kind=kLoop, calls=%fused_computation.54 | loop fusion | flops 6291456 | bytes 12582914 | tf_op jit(solution)/shard_map/jit(_where)/select_n | solution.py:32
  143.8 31.5 %collective-permute-done.9 = bf16[128,3072]{1,0:T(8,128)(2,1)S(1)} collective-permute-done((bf16[128,3072]{1,0:T(8,128)(2,1)}, bf16[128,3072]{1,0:T(8,128)(2,1)S(1)}, u32[]{:S(2)}, u32[]{:S(2)}) %collective-permute-start.9) | collective-permute-done | bytes 786464 | tf_op jit(solution)/shard_map/ppermute | solution.py:28
  175.5 1.9 pad_maximum_fusion.3
  177.9 15.9 %collective-permute-done.14 = bf16[64,3072]{1,0:T(8,128)(2,1)S(1)} collective-permute-done((bf16[64,3072]{1,0:T(8,128)(2,1)S(1)}, bf16[64,3072]{1,0:T(8,128)(2,1)S(1)}, u32[]{:S(2)}, u32[]{:S(2)}) %collective-permute-start.14) | collective-permute-done | bytes 393248 | tf_op jit(solution)/shard_map/ppermute | solution.py:28
  193.8 1.2 pad_maximum_fusion.6
  195.0 4.1 %fusion.33 = (bf16[128,6144]{1,0:T(8,128)(2,1)}, f32[128,6144]{1,0:T(8,128)}) fusion(bf16[128,6144]{1,0:T(8,128)(2,1)} %collective-permute-done.8, f32[2,128,6144]{2,1,0:T(8,128)S(1)} %bitcast.119, s32[]{:T(128)S(6)} %select_n.160), kind=kLoop, calls=%fused_computation.76 | loop fusion | flops 2359296 | bytes 9437188 | tf_op jit(solution)/shard_map/convert_element_type | solution.py:99
  199.6 1.2 fusion.29
  201.9 3.2 pad_maximum_fusion
  205.2 28.2 %convolution_convert_fusion = bf16[6144,3072]{1,0:T(8,128)(2,1)} fusion(bf16[512,6144]{1,0:T(8,128)(2,1)} %bitcast.124, bf16[512,3072]{1,0:T(8,128)(2,1)} %copy-done.1), kind=kOutput, calls=%fused_computation.7 | convolution fusion | flops 19346227200 | bytes 47185920 | tf_op jit(solution)/shard_map/dot_general | solution.py:42
  233.4 2.1 select_bitcast_fusion.1
  236.1 3.4 %copy.12 = bf16[2,2,128,6144]{3,2,1,0:T(8,128)(2,1)} copy(bf16[2,2,128,6144]{3,2,0,1:T(8,128)(2,1)S(1)} %pad_maximum_fusion.1) | data formatting | bytes 12582912 | tf_op jit(solution)/shard_map/concatenate | solution.py:34
  240.1 2.5 fusion.32
  242.6 19.3 %fusion.12 = bf16[192,6144]{1,0:T(8,128)(2,1)} fusion(bf16[192,3072]{1,0:T(8,128)(2,1)} %bitcast.141, bf16[1,6144,3072]{2,1,0:T(8,128)(2,1)} %param.5), kind=kOutput, calls=%fused_computation.17 | convolution fusion | flops 7248936960 | bytes 41287680 | tf_op jit(solution)/shard_map/dot_general | solution.py:38
  261.9 1.3 dynamic-slice_bitcast_fusion.2
  263.4 1.7 pad_maximum_fusion.4
  265.1 1.3 collective-permute-start.10
  266.4 5.6 %collective-permute-start.17 = (bf16[80,6144]{1,0:T(8,128)(2,1)}, bf16[80,6144]{1,0:T(8,128)(2,1)}, u32[]{:S(2)}, u32[]{:S(2)}) collective-permute-start(bf16[80,6144]{1,0:T(8,128)(2,1)} %get-tuple-element.52), channel_id=1, source_target_pairs={{0,4},{1,5},{2,6},{3,7},{12,8},{13,9},{14,10},{15,11},{16,20},{17,... | collective-permute-start | bytes 2949128 | tf_op jit(solution)/shard_map/ppermute | solution.py:99
  273.2 1.4 collective-permute-start.18
  274.6 34.5 %add_convert_fusion = bf16[6144,3072]{1,0:T(8,128)(2,1)} fusion(bf16[6144,3072]{1,0:T(8,128)(2,1)} %convolution_convert_fusion, bf16[512,6144]{1,0:T(8,128)(2,1)} %bitcast.123, bf16[512,3072]{1,0:T(8,128)(2,1)S(1)} %bitcast.131), kind=kOutput, calls=%fused_computation | convolution fusion | flops 19383975936 | bytes 84934656 | tf_op jit(solution)/shard_map/dot_general | solution.py:42
  309.3 1.3 collective-permute-start.19
  310.6 1.6 fusion.25
  312.2 10.9 %collective-permute-done.19 = bf16[48,6144]{1,0:T(8,128)(2,1)S(1)} collective-permute-done((bf16[48,6144]{1,0:T(8,128)(2,1)S(1)}, bf16[48,6144]{1,0:T(8,128)(2,1)S(1)}, u32[]{:S(2)}, u32[]{:S(2)}) %collective-permute-start.19) | collective-permute-done | bytes 589856 | tf_op jit(solution)/shard_map/ppermute | solution.py:99
  323.4 1.3 maximum_bitcast_fusion
  (74 shorter events, 7.8 us)
Async XLA Ops:
  0.6 7.4 %copy-start.10 = (bf16[1,512,3072]{2,1,0:T(8,128)(2,1)S(1)}, bf16[1,512,3072]{2,1,0:T(8,128)(2,1)}, u32[]{:S(2)}) copy-start(bf16[1,512,3072]{2,1,0:T(8,128)(2,1)} %param.7) | copy-start | bytes 9437188
  3.4 29.4 %collective-permute-start = (bf16[64,6144]{1,0:T(8,128)(2,1)}, bf16[64,6144]{1,0:T(8,128)(2,1)}, u32[]{:S(2)}, u32[]{:S(2)}) collective-permute-start(bf16[64,6144]{1,0:T(8,128)(2,1)} %get-tuple-element.67), channel_id=1, source_target_pairs={{0,4},{1,5},{2,6},{3,7},{4,0},{5,1},{6,2},{7,3},{8,12},{9,13},{10,... | collective-permute-start | bytes 2359304 | tf_op jit(solution)/shard_map/ppermute | solution.py:28
  6.5 26.3 %collective-permute-start.1 = (bf16[64,6144]{1,0:T(8,128)(2,1)}, bf16[64,6144]{1,0:T(8,128)(2,1)}, u32[]{:S(2)}, u32[]{:S(2)}) collective-permute-start(bf16[64,6144]{1,0:T(8,128)(2,1)} %get-tuple-element.67), channel_id=1, source_target_pairs={{0,2},{1,3},{2,0},{3,1},{4,6},{5,7},{6,4},{7,5},{8,10},{9,11},{10,... | collective-permute-start | bytes 2359304 | tf_op jit(solution)/shard_map/ppermute | solution.py:28
  13.8 57.4 %copy-start.1 = (bf16[512,3072]{1,0:T(8,128)(2,1)}, bf16[512,3072]{1,0:T(8,128)(2,1)S(1)}, u32[]{:S(2)}) copy-start(bf16[512,3072]{1,0:T(8,128)(2,1)S(1)} %fusion.22) | copy-start | bytes 9437188
  15.0 53.7 %collective-permute-start.4 = (bf16[192,3072]{1,0:T(8,128)(2,1)}, bf16[192,3072]{1,0:T(8,128)(2,1)}, u32[]{:S(2)}, u32[]{:S(2)}) collective-permute-start(bf16[192,3072]{1,0:T(8,128)(2,1)} %bitcast.8), channel_id=1, source_target_pairs={{0,8},{1,9},{2,10},{3,11},{4,12},{5,13},{6,14},{7,15},{8,0},{9,1},... | collective-permute-start | bytes 3538952 | tf_op jit(solution)/shard_map/ppermute | solution.py:28
  32.8 35.9 %collective-permute-start.2 = (bf16[64,6144]{1,0:T(8,128)(2,1)}, bf16[64,6144]{1,0:T(8,128)(2,1)}, u32[]{:S(2)}, u32[]{:S(2)}) collective-permute-start(bf16[64,6144]{1,0:T(8,128)(2,1)} %get-tuple-element.28), channel_id=1, source_target_pairs={{0,4},{1,5},{2,6},{3,7},{4,0},{5,1},{6,2},{7,3},{8,12},{9,13},{10,... | collective-permute-start | bytes 2359304 | tf_op jit(solution)/shard_map/ppermute | solution.py:28
  32.8 35.9 %collective-permute-start.3 = (bf16[64,6144]{1,0:T(8,128)(2,1)}, bf16[64,6144]{1,0:T(8,128)(2,1)}, u32[]{:S(2)}, u32[]{:S(2)}) collective-permute-start(bf16[64,6144]{1,0:T(8,128)(2,1)} %get-tuple-element.28), channel_id=1, source_target_pairs={{0,2},{1,3},{2,0},{3,1},{4,6},{5,7},{6,4},{7,5},{8,10},{9,11},{10,... | collective-permute-start | bytes 2359304 | tf_op jit(solution)/shard_map/ppermute | solution.py:28
  68.7 12.7 %slice-start.2 = ((s8[6291456]{0:T(1024)(128)(4,1)}), s8[4194304]{0:T(1024)(128)(4,1)S(1)}, s32[]{:S(2)}) async-start(s8[6291456]{0:T(1024)(128)(4,1)} %bitcast.126), calls=%async_computation.2 | async-start | bytes 8388608
  71.1 10.3 %slice-start.3 = ((s8[6291456]{0:T(1024)(128)(4,1)}), s8[2097152]{0:T(1024)(128)(4,1)S(1)}, s32[]{:S(2)}) async-start(s8[6291456]{0:T(1024)(128)(4,1)} %bitcast.126), calls=%async_computation.3 | async-start | bytes 4194304
  71.1 10.3 %collective-permute-start.7 = (bf16[2,128,6144]{2,1,0:T(8,128)(2,1)S(1)}, bf16[2,128,6144]{2,1,0:T(8,128)(2,1)S(1)}, u32[]{:S(2)}, u32[]{:S(2)}) collective-permute-start(bf16[2,128,6144]{2,1,0:T(8,128)(2,1)S(1)} %dynamic-slice_bitcast_fusion), channel_id=1, source_target_pairs={{0,1},{1,0},{2,3},{3,2},{4,5},{5,4},{6,7},{7,6},{8,9},{9,8},{10,11... | collective-permute-start | bytes 9437192 | tf_op jit(solution)/shard_map/ppermute | solution.py:28
  74.7 37.8 %collective-permute-start.5 = (bf16[128,3072]{1,0:T(8,128)(2,1)S(1)}, bf16[128,3072]{1,0:T(8,128)(2,1)S(1)}, u32[]{:S(2)}, u32[]{:S(2)}) collective-permute-start(bf16[128,3072]{1,0:T(8,128)(2,1)S(1)} %bitcast.142), channel_id=1, source_target_pairs={{0,8},{1,9},{2,10},{3,11},{4,12},{5,13},{6,14},{7,15},{8,0},{9,1},... | collective-permute-start | bytes 2359304 | tf_op jit(solution)/shard_map/ppermute | solution.py:28
  77.4 5.1 %copy-start.7 = (bf16[128,6144]{1,0:T(8,128)(2,1)}, bf16[128,6144]{1,0:T(8,128)(2,1)S(1)}, u32[]{:S(2)}) copy-start(bf16[128,6144]{1,0:T(8,128)(2,1)S(1)} %constant_dynamic-update-slice_fusion) | copy-start | bytes 4718596
  77.4 36.6 %collective-permute-start.6 = (bf16[128,6144]{1,0:T(8,128)(2,1)S(1)}, bf16[128,6144]{1,0:T(8,128)(2,1)S(1)}, u32[]{:S(2)}, u32[]{:S(2)}) collective-permute-start(bf16[128,6144]{1,0:T(8,128)(2,1)S(1)} %constant_dynamic-update-slice_fusion), channel_id=1, source_target_pairs={{0,2},{1,3},{2,0},{3,1},{4,6},{5,7},{6,4},{7,5},{8,10},{9,11},{10,... | collective-permute-start | bytes 4718600 | tf_op jit(solution)/shard_map/ppermute | solution.py:28
  80.2 1.2 copy-start.6
  82.5 35.8 %copy-start = (f32[2,128,6144]{2,1,0:T(8,128)}, f32[2,128,6144]{2,1,0:T(8,128)S(1)}, u32[]{:S(2)}) copy-start(f32[2,128,6144]{2,1,0:T(8,128)S(1)} %convert_add_fusion.1) | copy-start | bytes 18874372
  112.4 5.9 %copy-start.11 = (bf16[128,3072]{1,0:T(8,128)(2,1)}, bf16[128,3072]{1,0:T(8,128)(2,1)S(1)}, u32[]{:S(2)}) copy-start(bf16[128,3072]{1,0:T(8,128)(2,1)S(1)} %collective-permute-done.5) | copy-start | bytes 2359300
  114.0 3.0 copy-start.14
  115.4 79.6 %collective-permute-start.8 = (bf16[128,6144]{1,0:T(8,128)(2,1)}, bf16[128,6144]{1,0:T(8,128)(2,1)}, u32[]{:S(2)}, u32[]{:S(2)}) collective-permute-start(bf16[128,6144]{1,0:T(8,128)(2,1)} %fusion.26), channel_id=1, source_target_pairs={{0,2},{1,3},{2,0},{3,1},{4,6},{5,7},{6,4},{7,5},{8,10},{9,11},{10,... | collective-permute-start | bytes 4718600 | tf_op jit(solution)/shard_map/ppermute | solution.py:28
  138.8 36.5 %collective-permute-start.9 = (bf16[128,3072]{1,0:T(8,128)(2,1)}, bf16[128,3072]{1,0:T(8,128)(2,1)S(1)}, u32[]{:S(2)}, u32[]{:S(2)}) collective-permute-start(bf16[128,3072]{1,0:T(8,128)(2,1)} %bitcast.17), channel_id=1, source_target_pairs={{0,8},{1,9},{2,10},{3,11},{4,12},{5,13},{6,14},{7,15},{8,0},{9,1},... | collective-permute-start | bytes 2359304 | tf_op jit(solution)/shard_map/ppermute | solution.py:28
  143.4 31.9 %copy-start.5 = (bf16[320,6144]{1,0:T(8,128)(2,1)S(1)}, bf16[320,6144]{1,0:T(8,128)(2,1)}, u32[]{:S(2)}) copy-start(bf16[320,6144]{1,0:T(8,128)(2,1)} %fusion.9) | copy-start | bytes 11796484
  143.7 57.7 %collective-permute-start.11 = (bf16[2,128,6144]{2,1,0:T(8,128)(2,1)S(1)}, bf16[2,128,6144]{2,1,0:T(8,128)(2,1)S(1)}, u32[]{:S(2)}, u32[]{:S(2)}) collective-permute-start(bf16[2,128,6144]{2,1,0:T(8,128)(2,1)S(1)} %pad_maximum_fusion.2), channel_id=1, source_target_pairs={{0,1},{1,0},{2,3},{3,2},{4,5},{5,4},{6,7},{7,6},{8,9},{9,8},{10,11... | collective-permute-start | bytes 9437192 | tf_op jit(solution)/shard_map/ppermute | solution.py:28
  175.3 18.5 %copy-start.8 = (bf16[128,3072]{1,0:T(8,128)(2,1)}, bf16[128,3072]{1,0:T(8,128)(2,1)S(1)}, u32[]{:S(2)}) copy-start(bf16[128,3072]{1,0:T(8,128)(2,1)S(1)} %collective-permute-done.9) | copy-start | bytes 2359300
  175.3 18.5 %collective-permute-start.14 = (bf16[64,3072]{1,0:T(8,128)(2,1)S(1)}, bf16[64,3072]{1,0:T(8,128)(2,1)S(1)}, u32[]{:S(2)}, u32[]{:S(2)}) collective-permute-start(bf16[64,3072]{1,0:T(8,128)(2,1)S(1)} %bitcast.143), channel_id=1, source_target_pairs={{0,8},{1,9},{2,10},{3,11},{4,12},{5,13},{6,14},{7,15},{8,0},{9,1},... | collective-permute-start | bytes 1179656 | tf_op jit(solution)/shard_map/ppermute | solution.py:28
  175.3 19.7 %slice-start = ((s8[6291456]{0:T(1024)(128)(4,1)}), s8[4194304]{0:T(1024)(128)(4,1)S(1)}, s32[]{:S(2)}) async-start(s8[6291456]{0:T(1024)(128)(4,1)} %bitcast.118), calls=%async_computation | async-start | bytes 8388608
  175.5 23.7 %collective-permute-start.12 = (bf16[2,80,6144]{2,1,0:T(8,128)(2,1)S(1)}, bf16[2,80,6144]{2,1,0:T(8,128)(2,1)S(1)}, u32[]{:S(2)}, u32[]{:S(2)}) collective-permute-start(bf16[2,80,6144]{2,1,0:T(8,128)(2,1)S(1)} %dynamic-slice_bitcast_fusion.1), channel_id=1, source_target_pairs={{0,1},{1,0},{2,3},{3,2},{4,5},{5,4},{6,7},{7,6},{8,9},{9,8},{10,11... | collective-permute-start | bytes 5898248 | tf_op jit(solution)/shard_map/ppermute | solution.py:28
  175.5 19.5 %slice-start.1 = ((s8[6291456]{0:T(1024)(128)(4,1)}), s8[2097152]{0:T(1024)(128)(4,1)S(1)}, s32[]{:S(2)}) async-start(s8[6291456]{0:T(1024)(128)(4,1)} %bitcast.118), calls=%async_computation.1 | async-start | bytes 4194304
  177.5 56.0 %collective-permute-start.13 = (bf16[2,128,6144]{2,1,0:T(8,128)(2,1)}, bf16[2,128,6144]{2,1,0:T(8,128)(2,1)}, u32[]{:S(2)}, u32[]{:S(2)}) collective-permute-start(bf16[2,128,6144]{2,1,0:T(8,128)(2,1)} %pad_maximum_fusion.3), channel_id=1, source_target_pairs={{0,1},{1,0},{2,3},{3,2},{4,5},{5,4},{6,7},{7,6},{8,9},{9,8},{10,11... | collective-permute-start | bytes 9437192 | tf_op jit(solution)/shard_map/ppermute | solution.py:28
  193.8 5.3 %copy-start.15 = (bf16[64,3072]{1,0:T(8,128)(2,1)}, bf16[64,3072]{1,0:T(8,128)(2,1)S(1)}, u32[]{:S(2)}) copy-start(bf16[64,3072]{1,0:T(8,128)(2,1)S(1)} %collective-permute-done.14) | copy-start | bytes 1179652
  199.6 2.3 copy-start.3
  200.8 38.7 %collective-permute-start.15 = (bf16[80,6144]{1,0:T(8,128)(2,1)}, bf16[80,6144]{1,0:T(8,128)(2,1)}, u32[]{:S(2)}, u32[]{:S(2)}) collective-permute-start(bf16[80,6144]{1,0:T(8,128)(2,1)} %fusion.29), channel_id=1, source_target_pairs={{0,2},{1,3},{2,0},{3,1},{4,6},{5,7},{6,4},{7,5},{8,10},{9,11},{10,... | collective-permute-start | bytes 2949128 | tf_op jit(solution)/shard_map/ppermute | solution.py:28
  236.1 4.0 %copy-start.4 = (f32[2,80,6144]{2,1,0:T(8,128)S(1)}, f32[2,80,6144]{2,1,0:T(8,128)}, u32[]{:S(2)}) copy-start(f32[2,80,6144]{2,1,0:T(8,128)} %copy-done.3) | copy-start | bytes 11796484
  242.6 20.8 %copy-start.9 = (bf16[128,3072]{1,0:T(8,128)(2,1)S(1)}, bf16[128,3072]{1,0:T(8,128)(2,1)}, u32[]{:S(2)}) copy-start(bf16[128,3072]{1,0:T(8,128)(2,1)} %copy-done.8) | copy-start | bytes 2359300
  242.6 20.8 %copy-start.12 = (bf16[128,3072]{1,0:T(8,128)(2,1)S(1)}, bf16[128,3072]{1,0:T(8,128)(2,1)}, u32[]{:S(2)}) copy-start(bf16[128,3072]{1,0:T(8,128)(2,1)} %copy-done.11) | copy-start | bytes 2359300
  263.3 8.8 %copy-start.13 = (bf16[192,6144]{1,0:T(8,128)(2,1)S(1)}, bf16[192,6144]{1,0:T(8,128)(2,1)}, u32[]{:S(2)}) copy-start(bf16[192,6144]{1,0:T(8,128)(2,1)} %fusion.12) | copy-start | bytes 7077892
  263.3 8.8 %collective-permute-start.16 = (bf16[2,48,6144]{2,1,0:T(8,128)(2,1)S(1)}, bf16[2,48,6144]{2,1,0:T(8,128)(2,1)S(1)}, u32[]{:S(2)}, u32[]{:S(2)}) collective-permute-start(bf16[2,48,6144]{2,1,0:T(8,128)(2,1)S(1)} %dynamic-slice_bitcast_fusion.2), channel_id=1, source_target_pairs={{0,1},{1,0},{2,3},{3,2},{4,5},{5,4},{6,7},{7,6},{8,9},{9,8},{10,11... | collective-permute-start | bytes 3538952 | tf_op jit(solution)/shard_map/ppermute | solution.py:28
  265.1 44.0 %collective-permute-start.10 = (bf16[128,6144]{1,0:T(8,128)(2,1)}, bf16[128,6144]{1,0:T(8,128)(2,1)S(1)}, u32[]{:S(2)}, u32[]{:S(2)}) collective-permute-start(bf16[128,6144]{1,0:T(8,128)(2,1)} %get-tuple-element.54), channel_id=1, source_target_pairs={{4,0},{5,1},{6,2},{7,3},{8,12},{9,13},{10,14},{11,15},{20,16},{21,... | collective-permute-start | bytes 4718600 | tf_op jit(solution)/shard_map/ppermute | solution.py:99
  266.4 42.7 %collective-permute-start.17 = (bf16[80,6144]{1,0:T(8,128)(2,1)}, bf16[80,6144]{1,0:T(8,128)(2,1)}, u32[]{:S(2)}, u32[]{:S(2)}) collective-permute-start(bf16[80,6144]{1,0:T(8,128)(2,1)} %get-tuple-element.52), channel_id=1, source_target_pairs={{0,4},{1,5},{2,6},{3,7},{12,8},{13,9},{14,10},{15,11},{16,20},{17,... | collective-permute-start | bytes 2949128 | tf_op jit(solution)/shard_map/ppermute | solution.py:99
  273.2 35.9 %collective-permute-start.18 = (bf16[48,6144]{1,0:T(8,128)(2,1)}, bf16[48,6144]{1,0:T(8,128)(2,1)S(1)}, u32[]{:S(2)}, u32[]{:S(2)}) collective-permute-start(bf16[48,6144]{1,0:T(8,128)(2,1)} %fusion.31), channel_id=1, source_target_pairs={{0,2},{1,3},{2,0},{3,1},{4,6},{5,7},{6,4},{7,5},{8,10},{9,11},{10,... | collective-permute-start | bytes 1769480 | tf_op jit(solution)/shard_map/ppermute | solution.py:28
  274.6 36.0 %copy-start.2 = (f32[128,6144]{1,0:T(8,128)S(1)}, f32[128,6144]{1,0:T(8,128)}, u32[]{:S(2)}) copy-start(f32[128,6144]{1,0:T(8,128)} %get-tuple-element.55) | copy-start | bytes 9437188
  309.3 13.8 %collective-permute-start.19 = (bf16[48,6144]{1,0:T(8,128)(2,1)S(1)}, bf16[48,6144]{1,0:T(8,128)(2,1)S(1)}, u32[]{:S(2)}, u32[]{:S(2)}) collective-permute-start(bf16[48,6144]{1,0:T(8,128)(2,1)S(1)} %fusion.30), channel_id=1, source_target_pairs={{0,4},{1,5},{2,6},{3,7},{12,8},{13,9},{14,10},{15,11},{16,20},{17,... | collective-permute-start | bytes 1769480 | tf_op jit(solution)/shard_map/ppermute | solution.py:99
